TPU v7x, 256 devices: a whole 4x4x8 slice. The times are simulated.
256 devices in a mesh: seq: 32 (over y, z), mp: 8 (over x, core).
Axes of the slice: x: 4, y: 4, z: 8, core: 2. Of those that a mesh axis runs over, the one named last changes fastest.
Arguments:
- patch_hidden: bfloat16 [16384, 5120], P('seq', 'mp'), may hold values from -6 to 6
- out_weight: bfloat16 [5120, 8192], P(None, 'mp'), may hold values from -0.078125 to 0.078125
- out_bias: bfloat16 [8192], P('mp'), may hold values from -3 to 3
- cluster_ids: int32 [16384], P('seq'), may hold values from 0 to 8191, as said below
- memory_slots: bfloat16 [8192, 8192], P('seq', 'mp'), may hold values from -6 to 6
- slot_counts: int32 [8192], P('seq'), may hold values from 1 to 16
- norm_gain: bfloat16 [8192], P('mp'), may hold values from 0.099609375 to 1.8984375
- key_weight: bfloat16 [8192, 1024], P('seq', 'mp'), may hold values from -0.0625 to 0.0625
- value_weight: bfloat16 [8192, 1024], P('seq', 'mp'), may hold values from -0.0625 to 0.0625
- key_bias: bfloat16 [1024], P('mp'), may hold values from -3 to 3
- value_bias: bfloat16 [1024], P('mp'), may hold values from -3 to 3
Outputs:
- memory_new: bfloat16 [8192, 8192], P('seq', 'mp')
- slot_keys: bfloat16 [8192, 1024], P('seq', 'mp')
- slot_values: bfloat16 [8192, 1024], P('seq', 'mp')
Inputs may be any that keep to these rules, and one draw needn't show every extreme that they name: `cluster_ids`: slots s * 256 to (s + 1) * 256 - 1 belong to index s of seq. Of the 512 rows of one index of seq, at most 48 name slots of any one index of seq, and in every draw some index of seq receives exactly 48 rows from every index of seq.
All inputs are finite; a program needn't handle non-finite values.
Results may differ from a plain program's by a relative error of at most 0.0054.
Values may be sent and summed in bfloat16 or wider, within the bound.
A program may use at most 128 MiB of HBM per device.

v0:
```python
import jax
import jax.numpy as jnp
from jax import lax
from jax.sharding import PartitionSpec as P

D = 8192


def on_device(
    patch_hidden,
    out_weight,
    out_bias,
    cluster_ids,
    memory_slots,
    slot_counts,
    norm_gain,
    key_weight,
    value_weight,
    key_bias,
    value_bias,
):
    row_count = patch_hidden.shape[0]
    width_local = out_weight.shape[1]
    slot_local = memory_slots.shape[0]
    seq_count = lax.axis_size("seq")
    capacity = 3 * row_count // seq_count
    bias_wide = out_bias.astype(jnp.float32)
    owner = cluster_ids // slot_local
    owner_table = (owner[:, None] == jnp.arange(seq_count, dtype=jnp.int32)[None, :]).astype(
        jnp.int32
    )
    rank = jnp.sum(jnp.cumsum(owner_table, axis=0) * owner_table, axis=1) - 1
    target = owner * capacity + rank
    send_slots = (
        jnp.full((seq_count * capacity,), -1, jnp.int32).at[target].set(cluster_ids % slot_local)
    )
    activated = jax.nn.gelu(
        lax.all_gather(patch_hidden, "mp", axis=1, tiled=True).astype(jnp.float32),
        approximate=False,
    ).astype(jnp.bfloat16)
    projected = jnp.dot(activated, out_weight, preferred_element_type=jnp.float32)
    merged = projected + bias_wide[None, :]
    send_rows = jnp.zeros((seq_count * capacity, width_local), jnp.float32).at[target].set(merged)
    got_rows, got_slots = (
        lax.all_to_all(send_rows, "seq", split_axis=0, concat_axis=0, tiled=True),
        lax.all_to_all(send_slots, "seq", split_axis=0, concat_axis=0, tiled=True),
    )
    matches = jnp.arange(slot_local, dtype=jnp.int32)[:, None] == got_slots[None, :]
    totals = jnp.dot(
        matches.astype(jnp.float32),
        got_rows,
        precision=lax.Precision.HIGHEST,
        preferred_element_type=jnp.float32,
    )
    arrivals = jnp.sum(matches.astype(jnp.float32), axis=1)
    weight = slot_counts.astype(jnp.float32)
    memory_new = (
        (weight[:, None] * memory_slots.astype(jnp.float32) + totals) / (weight + arrivals)[:, None]
    ).astype(jnp.bfloat16)
    key_full, value_full = (
        lax.all_gather(key_weight, "seq", axis=0, tiled=True),
        lax.all_gather(value_weight, "seq", axis=0, tiled=True),
    )
    head_local = key_full.shape[1]
    stored = lax.optimization_barrier(memory_new).astype(jnp.float32)
    squares = lax.psum(jnp.sum(stored * stored, axis=1), "mp")
    inverse = lax.rsqrt(squares / D + 1e-06)
    normed = (stored * inverse[:, None] * norm_gain.astype(jnp.float32)[None, :]).astype(
        jnp.bfloat16
    )
    key_rows, value_rows = (
        lax.all_to_all(key_full, "mp", split_axis=0, concat_axis=1, tiled=True),
        lax.all_to_all(value_full, "mp", split_axis=0, concat_axis=1, tiled=True),
    )
    mp_count = key_rows.shape[1] // head_local
    joined = jnp.stack(
        [
            key_rows.reshape(width_local, mp_count, head_local),
            value_rows.reshape(width_local, mp_count, head_local),
        ],
        axis=2,
    ).reshape(width_local, 2 * mp_count * head_local)
    shared = lax.psum_scatter(
        lax.dot_general(
            joined, normed, (((0,), (1,)), ((), ())), preferred_element_type=jnp.float32
        ),
        "mp",
        scatter_dimension=0,
        tiled=True,
    )
    combined = shared.T
    key_part = combined[:, :head_local]
    value_part = combined[:, head_local:]
    slot_keys = (key_part + key_bias.astype(jnp.float32)[None, :]).astype(jnp.bfloat16)
    slot_values = (value_part + value_bias.astype(jnp.float32)[None, :]).astype(jnp.bfloat16)
    return (memory_new, slot_keys, slot_values)


def solution(mesh):
    return jax.shard_map(
        on_device,
        mesh=mesh,
        in_specs=(
            P("seq", "mp"),
            P(None, "mp"),
            P("mp"),
            P("seq"),
            P("seq", "mp"),
            P("seq"),
            P("mp"),
            P("seq", "mp"),
            P("seq", "mp"),
            P("mp"),
            P("mp"),
        ),
        out_specs=(P("seq", "mp"), P("seq", "mp"), P("seq", "mp")),
        check_vma=False,
    )
```

profile of v0, /device:TPU:8, one launch (start us, length us, event | category | flops | bytes accessed | tf_op | source)
XLA Modules:
  0.0 477.1 jit_solution(14380446403744334530)
XLA Ops:
  7.2 0.0 all-gather.8.cloned.1.call-start
  7.2 0.7 all-gather.8.cloned.1.call-update
  7.9 0.0 all-gather.6.cloned.1.call-start
  7.9 0.7 all-gather.6.cloned.1.call-update
  8.6 0.0 all-gather.4.cloned.1.call-start
  8.7 0.7 all-gather.4.cloned.1.call-update
  9.4 0.7 add_select_fusion
  10.1 1.2 reduce-window.6
  11.3 0.2 slice_reduce_fusion
  11.5 0.1 fusion.52
  11.6 2.5 scatter_custom_fusion
  14.1 0.1 all_to_all.38
  14.2 20.1 %all_to_all.53 = s32[32,48,1]{1,2,0:T(1,128)S(1)} all-to-all(s32[32,48,1]{1,2,0:T(1,128)S(1)} %bitcast.39), channel_id=1, replica_groups=mesh['seq'=32,'mp'=8] {'seq'}, dimensions={0} | all-to-all | bytes 12288 | tf_op jit(solution)/shard_map/all_to_all | solution.py:46
  34.3 55.9 %all-gather.8.cloned.1.call-done = bf16[8192,128]{1,0:T(8,128)(2,1)} async-done(((bf16[256,128]{1,0:T(8,128)(2,1)}), bf16[8192,128]{1,0:T(8,128)(2,1)}) %all-gather.8.cloned.1.call-update) | async-done | bytes 2097168 | tf_op jit(solution)/shard_map/all_gather | solution.py:62
  90.2 4.3 all-to-all-start.3
  94.5 0.7 convert_element_type.53
  95.2 72.8 %all-gather.6.cloned.1.call-done = bf16[8192,128]{1,0:T(8,128)(2,1)} async-done(((bf16[256,128]{1,0:T(8,128)(2,1)}), bf16[8192,128]{1,0:T(8,128)(2,1)}) %all-gather.6.cloned.1.call-update) | async-done | bytes 2097168 | tf_op jit(solution)/shard_map/all_gather | solution.py:61
  168.0 0.0 all-to-all-done.3
  168.0 4.4 all-to-all-start.2
  172.3 49.5 %all-gather.4.cloned.1.call-done = bf16[512,5120]{1,0:T(8,128)(2,1)} async-done(((bf16[512,640]{1,0:T(8,128)(2,1)}), bf16[512,5120]{1,0:T(8,128)(2,1)}) %all-gather.4.cloned.1.call-update) | async-done | bytes 5242896 | tf_op jit(solution)/shard_map/all_gather | solution.py:38
  221.8 31.9 %fusion.31 = f32[512,1024]{1,0:T(8,128)} fusion(bf16[5120,1024]{1,0:T(8,128)(2,1)} %param.12, bf16[512,5120]{1,0:T(8,128)(2,1)} %all-gather.4.cloned.1.call-done), kind=kOutput, calls=%fused_computation.36 | convolution fusion | flops 5541724160 | bytes 17825792 | tf_op jit(solution)/shard_map/dot_general | solution.py:41
  253.7 0.0 copy-start.1
  253.7 0.0 copy-start.2
  253.7 6.4 %scatter_custom_fusion.1 = f32[1536,1024]{1,0:T(8,128)} fusion(s32[512]{0:T(512)S(1)} %compare_select_fusion, f32[]{:T(128)} %constant.48.clone.1, f32[512,1024]{1,0:T(8,128)} %fusion.31, f32[1024]{0:T(1024)S(1)} %convert_element_type.53), kind=kCustom, calls=%fused_computation.38 | custom fusion | flops 524288 | bytes 8392708 | tf_op jit(solution)/shard_map/scatter | solution.py:43
  260.2 0.0 all-to-all-done.2
  260.2 7.3 %all-to-all-start.1 = ((f32[32,48,1024]{2,1,0:T(8,128)}), f32[32,48,1024]{2,1,0:T(8,128)}, u32[]{:S(2)}, u32[]{:S(2)}) async-start(f32[32,48,1024]{2,1,0:T(8,128)} %bitcast.33), calls=%async_computation.1 | async-start | bytes 12582912 | tf_op jit(solution)/shard_map/all_to_all | solution.py:45
  267.5 0.0 copy-start.3
  267.5 0.0 reduce-scatter.2.cloned.1.call-start
  267.6 0.0 copy-done.1
  267.6 0.0 copy-done.2
  267.6 0.5 broadcast.74
  268.1 0.7 reduce.5
  268.8 0.1 eq.48
  268.9 0.2 convert_reduce_fusion
  269.2 3.9 pad_maximum_fusion
  273.1 6.5 %copy.30 = bf16[1024,8,2,128]{0,3,2,1:T(8,128)(2,1)} copy(bf16[1024,8,2,128]{3,0,1,2:T(8,128)(2,1)} %pad_maximum_fusion) | data formatting | bytes 8388608 | tf_op jit(solution)/shard_map/stack | solution.py:76
  279.5 0.0 copy-start.4
  279.5 0.0 copy-start.5
  279.5 128.1 %all-to-all-done.1 = f32[32,48,1024]{2,1,0:T(8,128)} async-done(((f32[32,48,1024]{2,1,0:T(8,128)}), f32[32,48,1024]{2,1,0:T(8,128)}, u32[]{:S(2)}, u32[]{:S(2)}) %all-to-all-start.1) | async-done | bytes 6291488 | tf_op jit(solution)/shard_map/all_to_all | solution.py:45
  407.6 0.0 copy-done.3
  407.6 6.3 %fusion.39 = bf16[256,1024]{1,0:T(8,128)(2,1)S(1)} fusion(f32[1536,1024]{1,0:T(8,128)} %bitcast.4, bf16[256,1024]{1,0:T(8,128)(2,1)S(1)} %copy-done.3, s32[1536]{0:T(1024)S(1)} %eq.48, f32[256]{0:T(256)S(1)} %convert_add_fusion, f32[256]{0:T(256)S(1)} %convert_element_type.48), kind=kOutput, calls=%fused_computation.48 | convolution fusion | flops 4833542144 | bytes 7348224 | tf_op jit(solution)/shard_map/dot_general | solution.py:49
  413.9 0.0 copy-start
  413.9 0.2 fusion.40
  414.1 12.4 %psum.7 = f32[256]{0:T(256)S(1)} all-reduce(f32[256]{0:T(256)S(1)} %fusion.40), channel_id=1, replica_groups=mesh['seq'=32,'mp'=8] {'mp'}, use_global_device_ids=true, to_apply=%region_7.8 | all-reduce | flops 256 | bytes 2048 | tf_op jit(solution)/shard_map/psum | solution.py:66
  426.5 4.9 %fusion.45 = f32[2048,256]{1,0:T(8,128)} fusion(bf16[1024,2048]{0,1:T(8,128)(2,1)} %bitcast.35, bf16[256,1024]{1,0:T(8,128)(2,1)S(1)} %fusion.39, f32[1024]{0:T(1024)S(1)} %convert_element_type.57, f32[256]{0:T(256)S(1)} %add_rsqrt_fusion), kind=kOutput, calls=%fused_computation.54 | convolution fusion | flops 1074790400 | bytes 6820864 | tf_op jit(solution)/shard_map/dot_general | solution.py:84
  431.4 0.0 reduce-scatter.2.cloned.1.call-update
  431.4 0.0 copy-done.4
  431.5 0.0 copy-done.5
  431.5 36.5 %reduce-scatter.2.cloned.1.call-done = f32[256,256]{1,0:T(8,128)} async-done(((f32[2048,256]{1,0:T(8,128)}), f32[256,256]{1,0:T(8,128)}) %reduce-scatter.2.cloned.1.call-update) | async-done | bytes 262160 | tf_op jit(solution)/shard_map/reduce_scatter | solution.py:83
  468.0 1.1 fusion.49
  469.1 0.7 copy.31
  469.8 0.7 copy.32
  470.6 0.0 copy-done
  (10 shorter events, 0.1 us)
Async XLA Ops:
  7.2 83.1 %all-gather.8.cloned.1.call-start = ((), (), s32[]{:S(2)}) async-start(), calls=%async_computation.7 | async-start | bytes 2162688 | tf_op jit(solution)/shard_map/all_gather | solution.py:62
  7.9 160.1 %all-gather.6.cloned.1.call-start = ((), (), s32[]{:S(2)}) async-start(), calls=%async_computation.6 | async-start | bytes 2162688 | tf_op jit(solution)/shard_map/all_gather | solution.py:61
  8.6 213.2 %all-gather.4.cloned.1.call-start = ((), (), s32[]{:S(2)}) async-start(), calls=%async_computation.5 | async-start | bytes 5898240 | tf_op jit(solution)/shard_map/all_gather | solution.py:38
  90.2 77.7 %all-to-all-start.3 = ((bf16[8,1024,128]{2,1,0:T(8,128)(2,1)}), bf16[8,1024,128]{2,1,0:T(8,128)(2,1)S(1)}, u32[]{:S(2)}, u32[]{:S(2)}) async-start(bf16[8,1024,128]{2,1,0:T(8,128)(2,1)} %bitcast.37), calls=%async_computation.3 | async-start | bytes 4194304 | tf_op jit(solution)/shard_map/all_to_all | solution.py:73
  168.0 92.2 %all-to-all-start.2 = ((bf16[8,1024,128]{2,1,0:T(8,128)(2,1)}), bf16[8,1024,128]{2,1,0:T(8,128)(2,1)}, u32[]{:S(2)}, u32[]{:S(2)}) async-start(bf16[8,1024,128]{2,1,0:T(8,128)(2,1)} %bitcast.36), calls=%async_computation.2 | async-start | bytes 4194304 | tf_op jit(solution)/shard_map/all_to_all | solution.py:72
  253.7 13.9 %copy-start.1 = (s32[256]{0:T(256)S(1)}, s32[256]{0:T(256)}, u32[]{:S(2)}) copy-start(s32[256]{0:T(256)} %param.16) | copy-start | bytes 3076
  253.7 13.9 %copy-start.2 = (bf16[1024]{0:T(1024)(128)(2,1)S(1)}, bf16[1024]{0:T(1024)(128)(2,1)}, u32[]{:S(2)}) copy-start(bf16[1024]{0:T(1024)(128)(2,1)} %param.17) | copy-start | bytes 6148
  260.2 147.4 %all-to-all-start.1 = ((f32[32,48,1024]{2,1,0:T(8,128)}), f32[32,48,1024]{2,1,0:T(8,128)}, u32[]{:S(2)}, u32[]{:S(2)}) async-start(f32[32,48,1024]{2,1,0:T(8,128)} %bitcast.33), calls=%async_computation.1 | async-start | bytes 12582912 | tf_op jit(solution)/shard_map/all_to_all | solution.py:45
  267.5 140.1 %copy-start.3 = (bf16[256,1024]{1,0:T(8,128)(2,1)S(1)}, bf16[256,1024]{1,0:T(8,128)(2,1)}, u32[]{:S(2)}) copy-start(bf16[256,1024]{1,0:T(8,128)(2,1)} %param.15) | copy-start | bytes 1572868
  267.5 200.5 %reduce-scatter.2.cloned.1.call-start = ((), (), s32[]{:S(2)}) async-start(), calls=%async_computation.8 | async-start | bytes 2359296 | tf_op jit(solution)/shard_map/reduce_scatter | solution.py:83
  279.5 151.9 %copy-start.4 = (bf16[128]{0:T(256)(128)(2,1)S(1)}, bf16[128]{0:T(256)(128)(2,1)}, u32[]{:S(2)}) copy-start(bf16[128]{0:T(256)(128)(2,1)} %param.21) | copy-start | bytes 772
  279.5 151.9 %copy-start.5 = (bf16[128]{0:T(256)(128)(2,1)S(1)}, bf16[128]{0:T(256)(128)(2,1)}, u32[]{:S(2)}) copy-start(bf16[128]{0:T(256)(128)(2,1)} %param.20) | copy-start | bytes 772
  413.9 56.7 %copy-start = (bf16[256,1024]{1,0:T(8,128)(2,1)}, bf16[256,1024]{1,0:T(8,128)(2,1)S(1)}, u32[]{:S(2)}) copy-start(bf16[256,1024]{1,0:T(8,128)(2,1)S(1)} %fusion.39) | copy-start | bytes 1572868
Sparse Core Ops, SparseCore 0:
  10.6 79.5 all-gather.7
  92.8 75.0 all-gather.5
  169.8 51.9 all-gather.3
  431.6 36.4 reduce-scatter.1
where the time goes:
time: 478 us; the launch traced here: 477 us
  waiting for transfers between devices  345 us (72%)
  matrix products  43.1 us (9%)
  blocking collectives  32.6 us (7%)
  starting transfers between devices  16.1 us (3%)
  other arithmetic  15.2 us (3%)
  between operations  13.9 us (3%)
  local copies, waits for them, and re-layouts  11.3 us (2%)
    all_to_all x1, waiting for transfers between devices, on_device(): lax.all_to_all(send_rows, 'seq', split_axis=0, concat_axis=0, tiled=True)  128 us
    all_gather x1, waiting for transfers between devices, on_device(): lax.all_gather(key_weight, 'seq', axis=0, tiled=True)  72.8 us
    all_gather x1, waiting for transfers between devices, on_device(): lax.all_gather(value_weight, 'seq', axis=0, tiled=True)  55.9 us
    all_gather x1, waiting for transfers between devices, on_device(): lax.all_gather(patch_hidden, 'mp', axis=1, tiled=True).astype(jnp.float32)  49.5 us
    reduce_scatter x1, waiting for transfers between devices, on_device(): lax.psum_scatter(lax.dot_general(joined, normed, (((0,), (1,)), ((), ()))...  36.5 us
    dot_general x1, matrix products, on_device(): jnp.dot(activated, out_weight, preferred_element_type=jnp.float32)  31.9 us
    all_to_all x1, blocking collectives, on_device(): lax.all_to_all(send_slots, 'seq', split_axis=0, concat_axis=0, tiled=True)  20.1 us
    psum x1, blocking collectives, on_device(): squares = lax.psum(jnp.sum(stored * stored, axis=1), 'mp')  12.4 us
  transfers between devices with their start and end apart: 7, of which 5 were waited for; matrix products, arithmetic and copies ran while one was open for 12% of the time, Pallas kernels for 0%

commit v1 on v0

--- a/solution.py
+++ b/solution.py
@@ -4,6 +4,28 @@
 from jax.sharding import PartitionSpec as P
 
 D = 8192
+
+
+def in_order(tiles, dim):
+    tiles = jnp.moveaxis(tiles, 0, dim)
+    lengths = tiles.shape
+    return tiles.reshape(*lengths[:dim], lengths[dim] * lengths[dim + 1], *lengths[dim + 2 :])
+
+
+def grow_blocks(shard, axis):
+    count = lax.axis_size(axis)
+    blocks = shard[None]
+    for level in range(count.bit_length() - 1):
+        bit = 1 << level
+        partner_block = lax.ppermute(blocks, axis, [(i, i ^ bit) for i in range(count)])
+        both = jnp.stack([blocks, partner_block])
+        upper = lax.axis_index(axis) >> level & 1
+        blocks = jnp.where(upper == 0, both, both[::-1]).reshape(-1, *shard.shape)
+    return blocks
+
+
+def gather_by_bits(x, axis, dim):
+    return in_order(grow_blocks(x, axis), dim)
 
 
 def on_device(
@@ -59,7 +81,7 @@
     ).astype(jnp.bfloat16)
     key_full, value_full = (
         lax.all_gather(key_weight, "seq", axis=0, tiled=True),
-        lax.all_gather(value_weight, "seq", axis=0, tiled=True),
+        gather_by_bits(value_weight, "seq", 0),
     )
     head_local = key_full.shape[1]
     stored = lax.optimization_barrier(memory_new).astype(jnp.float32)

time: 478 us -> 409 us (0.86)
  waiting for transfers between devices: 345 us -> 265 us
  starting transfers between devices: 16.1 us -> 43 us
  blocking collectives: 32.6 us -> 13.1 us
    all_gather x1, waiting for transfers between devices: 72.8 us -> 0.01 us  [on_device(): lax.all_gather(key_weight, 'seq', axis=0, tiled=True)]
    all_gather x1 -> x0, waiting for transfers between devices: 55.9 us -> none  [on_device(): lax.all_gather(value_weight, 'seq', axis=0, tiled=True)]
    ppermute x0 -> x5, waiting for transfers between devices: none -> 41.4 us  [grow_blocks(): lax.ppermute(blocks, axis, [(i, i ^ bit) for i in range(count)])]
    all_to_all x1, waiting for transfers between devices: 0.01 us -> 30.2 us  [on_device(): lax.all_to_all(value_full, 'mp', split_axis=0, concat_axis=1, tiled=True)]
    all_gather x1, waiting for transfers between devices: 49.5 us -> 27.9 us  [on_device(): lax.all_gather(patch_hidden, 'mp', axis=1, tiled=True).astype(jnp.float32)]
    all_to_all x1 -> x0, blocking collectives: 20.1 us -> none  [on_device(): lax.all_to_all(send_slots, 'seq', split_axis=0, concat_axis=0, tiled=True)]
    ppermute x0 -> x5, starting transfers between devices: none -> 17.7 us  [grow_blocks(): lax.ppermute(blocks, axis, [(i, i ^ bit) for i in range(count)])]
    all_to_all x0 -> x1, starting transfers between devices: none -> 6.29 us  [on_device(): lax.all_to_all(send_slots, 'seq', split_axis=0, concat_axis=0, tiled=True)]
  transfers between devices with their start and end apart: 7 -> 12, of which waited for: 5 -> 9; matrix products, arithmetic and copies ran while one was open for 12% -> 14% of each run, Pallas kernels for 0% -> 0%
where the time goes in v1:
time: 409 us; the launch traced here: 408 us
  waiting for transfers between devices  265 us (65%)
  matrix products  43.1 us (11%)
  starting transfers between devices  43 us (11%)
  other arithmetic  18.2 us (4%)
  between operations  14 us (3%)
  blocking collectives  13.1 us (3%)
  local copies, waits for them, and re-layouts  11.9 us (3%)
    all_to_all x1, waiting for transfers between devices, on_device(): lax.all_to_all(send_rows, 'seq', split_axis=0, concat_axis=0, tiled=True)  128 us
    ppermute x5, waiting for transfers between devices, grow_blocks(): lax.ppermute(blocks, axis, [(i, i ^ bit) for i in range(count)])  41.4 us
    reduce_scatter x1, waiting for transfers between devices, on_device(): lax.psum_scatter(lax.dot_general(joined, normed, (((0,), (1,)), ((), ()))...  35.7 us
    dot_general x1, matrix products, on_device(): jnp.dot(activated, out_weight, preferred_element_type=jnp.float32)  31.9 us
    all_to_all x1, waiting for transfers between devices, on_device(): lax.all_to_all(value_full, 'mp', split_axis=0, concat_axis=1, tiled=True)  30.2 us
    all_gather x1, waiting for transfers between devices, on_device(): lax.all_gather(patch_hidden, 'mp', axis=1, tiled=True).astype(jnp.float32)  27.9 us
    ppermute x5, starting transfers between devices, grow_blocks(): lax.ppermute(blocks, axis, [(i, i ^ bit) for i in range(count)])  17.7 us
    psum x1, blocking collectives, on_device(): squares = lax.psum(jnp.sum(stored * stored, axis=1), 'mp')  13.1 us
  transfers between devices with their start and end apart: 12, of which 9 were waited for; matrix products, arithmetic and copies ran while one was open for 14% of the time, Pallas kernels for 0%

profile of v1, /device:TPU:8, one launch (start us, length us, event | category | flops | bytes accessed | tf_op | source)
XLA Modules:
  0.0 407.8 jit_solution(1364474832576688557)
XLA Ops:
  7.2 0.0 all-gather.5.cloned.1.call-start
  7.2 0.7 all-gather.5.cloned.1.call-update
  7.9 0.0 all-gather.3.cloned.1.call-start
  7.9 0.7 all-gather.3.cloned.1.call-update
  8.7 2.0 collective-permute-start
  10.7 2.6 collective-permute-done
  13.2 0.9 pad_maximum_fusion.5
  14.1 3.4 collective-permute-start.1
  17.5 5.3 %collective-permute-done.1 = bf16[2,256,128]{2,1,0:T(8,128)(2,1)S(1)} collective-permute-done((bf16[2,256,128]{2,1,0:T(8,128)(2,1)S(1)}, bf16[2,256,128]{2,1,0:T(8,128)(2,1)S(1)}, u32[]{:S(2)}, u32[]{:S(2)}) %collective-permute-start.1) | collective-permute-done | bytes 131104 | tf_op jit(solution)/shard_map/ppermute | solution.py:20
  22.9 0.1 reverse_select_fusion.3
  22.9 6.5 %collective-permute-start.2 = (bf16[4,256,128]{2,1,0:T(8,128)(2,1)S(1)}, bf16[4,256,128]{2,1,0:T(8,128)(2,1)S(1)}, u32[]{:S(2)}, u32[]{:S(2)}) collective-permute-start(bf16[4,256,128]{2,1,0:T(8,128)(2,1)S(1)} %bitcast.58), channel_id=1, source_target_pairs={{0,32},{8,40},{16,48},{24,56},{32,0},{40,8},{48,16},{56,24},{64,96... | collective-permute-start | bytes 786440 | tf_op jit(solution)/shard_map/ppermute | solution.py:20
  29.4 12.2 %collective-permute-done.2 = bf16[4,256,128]{2,1,0:T(8,128)(2,1)S(1)} collective-permute-done((bf16[4,256,128]{2,1,0:T(8,128)(2,1)S(1)}, bf16[4,256,128]{2,1,0:T(8,128)(2,1)S(1)}, u32[]{:S(2)}, u32[]{:S(2)}) %collective-permute-start.2) | collective-permute-done | bytes 262176 | tf_op jit(solution)/shard_map/ppermute | solution.py:20
  41.6 0.1 pad_maximum_fusion.3
  41.7 0.1 reverse_select_fusion.2
  41.8 0.5 collective-permute-start.3
  42.3 9.1 %collective-permute-done.3 = bf16[8,256,128]{2,1,0:T(8,128)(2,1)S(1)} collective-permute-done((bf16[8,256,128]{2,1,0:T(8,128)(2,1)S(1)}, bf16[8,256,128]{2,1,0:T(8,128)(2,1)S(1)}, u32[]{:S(2)}, u32[]{:S(2)}) %collective-permute-start.3) | collective-permute-done | bytes 524320 | tf_op jit(solution)/shard_map/ppermute | solution.py:20
  51.4 0.1 pad_maximum_fusion.2
  51.5 0.3 reverse_select_fusion.1
  51.7 5.3 %collective-permute-start.4 = (bf16[16,256,128]{2,1,0:T(8,128)(2,1)S(1)}, bf16[16,256,128]{2,1,0:T(8,128)(2,1)S(1)}, u32[]{:S(2)}, u32[]{:S(2)}) collective-permute-start(bf16[16,256,128]{2,1,0:T(8,128)(2,1)S(1)} %bitcast.53), channel_id=1, source_target_pairs={{0,128},{8,136},{16,144},{24,152},{32,160},{40,168},{48,176},{56,1... | collective-permute-start | bytes 3145736 | tf_op jit(solution)/shard_map/ppermute | solution.py:20
  57.1 0.7 add_select_fusion
  57.8 1.2 reduce-window.6
  59.0 0.2 slice_reduce_fusion
  59.2 0.1 fusion.54
  59.4 2.5 scatter_custom_fusion
  61.8 0.7 all_to_all.38
  62.5 6.3 %all-to-all-start = ((s32[32,48,1]{1,2,0:T(1,128)}), s32[32,48,1]{1,2,0:T(1,128)S(1)}, u32[]{:S(2)}, u32[]{:S(2)}) async-start(s32[32,48,1]{1,2,0:T(1,128)} %bitcast.2), calls=%async_computation | async-start | bytes 32768 | tf_op jit(solution)/shard_map/all_to_all | solution.py:68
  68.8 12.2 %collective-permute-done.4 = bf16[16,256,128]{2,1,0:T(8,128)(2,1)S(1)} collective-permute-done((bf16[16,256,128]{2,1,0:T(8,128)(2,1)S(1)}, bf16[16,256,128]{2,1,0:T(8,128)(2,1)S(1)}, u32[]{:S(2)}, u32[]{:S(2)}) %collective-permute-start.4) | collective-permute-done | bytes 1048608 | tf_op jit(solution)/shard_map/ppermute | solution.py:20
  81.0 0.2 pad_maximum_fusion.1
  81.2 1.9 reverse_select_fusion
  83.1 0.0 all-to-all-done
  83.1 4.3 %all-to-all-start.3 = ((bf16[8,1024,128]{2,1,0:T(8,128)(2,1)}), bf16[8,1024,128]{2,1,0:T(8,128)(2,1)S(1)}, u32[]{:S(2)}, u32[]{:S(2)}) async-start(bf16[8,1024,128]{2,1,0:T(8,128)(2,1)} %bitcast.23), calls=%async_computation.3 | async-start | bytes 4194304 | tf_op jit(solution)/shard_map/all_to_all | solution.py:95
  87.4 0.0 copy-done.2
  87.4 30.2 %all-to-all-done.3 = bf16[8,1024,128]{2,1,0:T(8,128)(2,1)S(1)} async-done(((bf16[8,1024,128]{2,1,0:T(8,128)(2,1)}), bf16[8,1024,128]{2,1,0:T(8,128)(2,1)S(1)}, u32[]{:S(2)}, u32[]{:S(2)}) %all-to-all-start.3) | async-done | bytes 2097184 | tf_op jit(solution)/shard_map/all_to_all | solution.py:95
  117.6 4.4 %all-to-all-start.2 = ((bf16[8,1024,128]{2,1,0:T(8,128)(2,1)}), bf16[8,1024,128]{2,1,0:T(8,128)(2,1)}, u32[]{:S(2)}, u32[]{:S(2)}) async-start(bf16[8,1024,128]{2,1,0:T(8,128)(2,1)} %bitcast.55), calls=%async_computation.2 | async-start | bytes 4194304 | tf_op jit(solution)/shard_map/all_to_all | solution.py:94
  122.0 27.9 %all-gather.3.cloned.1.call-done = bf16[512,5120]{1,0:T(8,128)(2,1)} async-done(((bf16[512,640]{1,0:T(8,128)(2,1)}), bf16[512,5120]{1,0:T(8,128)(2,1)}) %all-gather.3.cloned.1.call-update) | async-done | bytes 5242896 | tf_op jit(solution)/shard_map/all_gather | solution.py:60
  149.9 31.9 %fusion.31 = f32[512,1024]{1,0:T(8,128)} fusion(bf16[5120,1024]{1,0:T(8,128)(2,1)} %param.12, bf16[512,5120]{1,0:T(8,128)(2,1)} %all-gather.3.cloned.1.call-done), kind=kOutput, calls=%fused_computation.36 | convolution fusion | flops 5541724160 | bytes 17825792 | tf_op jit(solution)/shard_map/dot_general | solution.py:63
  181.8 6.4 %scatter_custom_fusion.1 = f32[1536,1024]{1,0:T(8,128)} fusion(s32[512]{0:T(512)S(1)} %compare_select_fusion, f32[]{:T(128)} %constant.53.clone.1, f32[512,1024]{1,0:T(8,128)} %fusion.31, f32[1024]{0:T(1024)S(1)} %convert_element_type.53), kind=kCustom, calls=%fused_computation.39 | custom fusion | flops 524288 | bytes 8392708 | tf_op jit(solution)/shard_map/scatter | solution.py:65
  188.2 0.0 all-to-all-done.2
  188.2 10.2 %all-to-all-start.1 = ((f32[32,48,1024]{2,1,0:T(8,128)}), f32[32,48,1024]{2,1,0:T(8,128)}, u32[]{:S(2)}, u32[]{:S(2)}) async-start(f32[32,48,1024]{2,1,0:T(8,128)} %bitcast.50), calls=%async_computation.1 | async-start | bytes 12582912 | tf_op jit(solution)/shard_map/all_to_all | solution.py:67
  198.5 0.0 copy-start.4
  198.5 0.0 reduce-scatter.2.cloned.1.call-start
  198.5 0.0 copy-done.1
  198.6 0.0 copy-done.3
  198.6 0.5 broadcast.74
  199.1 0.7 reduce.5
  199.8 0.1 eq.63
  199.9 0.2 convert_reduce_fusion
  200.1 3.9 pad_maximum_fusion
  204.0 6.5 %copy.30 = bf16[1024,8,2,128]{0,3,2,1:T(8,128)(2,1)} copy(bf16[1024,8,2,128]{3,0,1,2:T(8,128)(2,1)} %pad_maximum_fusion) | data formatting | bytes 8388608 | tf_op jit(solution)/shard_map/stack | solution.py:98
  210.5 128.1 %all-to-all-done.1 = f32[32,48,1024]{2,1,0:T(8,128)} async-done(((f32[32,48,1024]{2,1,0:T(8,128)}), f32[32,48,1024]{2,1,0:T(8,128)}, u32[]{:S(2)}, u32[]{:S(2)}) %all-to-all-start.1) | async-done | bytes 6291488 | tf_op jit(solution)/shard_map/all_to_all | solution.py:67
  338.6 0.0 copy-done.4
  338.6 6.3 %fusion.39 = bf16[256,1024]{1,0:T(8,128)(2,1)S(1)} fusion(f32[1536,1024]{1,0:T(8,128)} %bitcast.4, bf16[256,1024]{1,0:T(8,128)(2,1)S(1)} %copy-done.4, s32[1536]{0:T(1024)S(1)} %eq.63, f32[256]{0:T(256)S(1)} %convert_add_fusion, f32[256]{0:T(256)S(1)} %convert_element_type.48), kind=kOutput, calls=%fused_computation.51 | convolution fusion | flops 4833542144 | bytes 7348224 | tf_op jit(solution)/shard_map/dot_general | solution.py:71
  344.8 0.0 copy-start
  344.8 0.2 fusion.40
  345.0 13.1 %psum.7 = f32[256]{0:T(256)S(1)} all-reduce(f32[256]{0:T(256)S(1)} %fusion.40), channel_id=1, replica_groups=mesh['seq'=32,'mp'=8] {'mp'}, use_global_device_ids=true, to_apply=%region_7.8 | all-reduce | flops 256 | bytes 2048 | tf_op jit(solution)/shard_map/psum | solution.py:88
  358.1 4.9 %fusion.45 = f32[2048,256]{1,0:T(8,128)} fusion(bf16[1024,2048]{0,1:T(8,128)(2,1)} %bitcast.52, bf16[256,1024]{1,0:T(8,128)(2,1)S(1)} %fusion.39, f32[1024]{0:T(1024)S(1)} %convert_element_type.57, f32[256]{0:T(256)S(1)} %add_rsqrt_fusion), kind=kOutput, calls=%fused_computation.59 | convolution fusion | flops 1074790400 | bytes 6820864 | tf_op jit(solution)/shard_map/dot_general | solution.py:106
  363.0 0.0 reduce-scatter.2.cloned.1.call-update
  363.0 0.0 copy-done.5
  363.1 0.0 copy-done.6
  363.1 35.7 %reduce-scatter.2.cloned.1.call-done = f32[256,256]{1,0:T(8,128)} async-done(((f32[2048,256]{1,0:T(8,128)}), f32[256,256]{1,0:T(8,128)}) %reduce-scatter.2.cloned.1.call-update) | async-done | bytes 262160 | tf_op jit(solution)/shard_map/reduce_scatter | solution.py:105
  398.8 1.1 fusion.49
  399.8 0.7 copy.31
  400.6 0.7 copy.32
  401.3 0.0 copy-done
  (19 shorter events, 0.2 us)
Async XLA Ops:
  7.2 110.5 %all-gather.5.cloned.1.call-start = ((), (), s32[]{:S(2)}) async-start(), calls=%async_computation.6 | async-start | bytes 2162688 | tf_op jit(solution)/shard_map/all_gather | solution.py:83
  7.9 142.0 %all-gather.3.cloned.1.call-start = ((), (), s32[]{:S(2)}) async-start(), calls=%async_computation.5 | async-start | bytes 5898240 | tf_op jit(solution)/shard_map/all_gather | solution.py:60
  8.7 4.6 %collective-permute-start = (bf16[1,256,128]{2,1,0:T(8,128)(2,1)}, bf16[1,256,128]{2,1,0:T(8,128)(2,1)S(1)}, u32[]{:S(2)}, u32[]{:S(2)}) collective-permute-start(bf16[1,256,128]{2,1,0:T(8,128)(2,1)} %bitcast.65), channel_id=1, source_target_pairs={{0,8},{8,0},{16,24},{24,16},{32,40},{40,32},{48,56},{56,48},{64,72... | collective-permute-start | bytes 196616 | tf_op jit(solution)/shard_map/ppermute | solution.py:20
  13.2 74.2 %copy-start.2 = (bf16[1024]{0:T(1024)(128)(2,1)S(1)}, bf16[1024]{0:T(1024)(128)(2,1)}, u32[]{:S(2)}) copy-start(bf16[1024]{0:T(1024)(128)(2,1)} %param.13) | copy-start | bytes 6148
  14.1 8.7 %collective-permute-start.1 = (bf16[2,256,128]{2,1,0:T(8,128)(2,1)S(1)}, bf16[2,256,128]{2,1,0:T(8,128)(2,1)S(1)}, u32[]{:S(2)}, u32[]{:S(2)}) collective-permute-start(bf16[2,256,128]{2,1,0:T(8,128)(2,1)S(1)} %get-tuple-element.21), channel_id=1, source_target_pairs={{0,16},{8,24},{16,0},{24,8},{32,48},{40,56},{48,32},{56,40},{64,80... | collective-permute-start | bytes 393224 | tf_op jit(solution)/shard_map/ppermute | solution.py:20
  22.9 18.7 %collective-permute-start.2 = (bf16[4,256,128]{2,1,0:T(8,128)(2,1)S(1)}, bf16[4,256,128]{2,1,0:T(8,128)(2,1)S(1)}, u32[]{:S(2)}, u32[]{:S(2)}) collective-permute-start(bf16[4,256,128]{2,1,0:T(8,128)(2,1)S(1)} %bitcast.58), channel_id=1, source_target_pairs={{0,32},{8,40},{16,48},{24,56},{32,0},{40,8},{48,16},{56,24},{64,96... | collective-permute-start | bytes 786440 | tf_op jit(solution)/shard_map/ppermute | solution.py:20
  41.8 9.6 %collective-permute-start.3 = (bf16[8,256,128]{2,1,0:T(8,128)(2,1)S(1)}, bf16[8,256,128]{2,1,0:T(8,128)(2,1)S(1)}, u32[]{:S(2)}, u32[]{:S(2)}) collective-permute-start(bf16[8,256,128]{2,1,0:T(8,128)(2,1)S(1)} %bitcast.56), channel_id=1, source_target_pairs={{0,64},{8,72},{16,80},{24,88},{32,96},{40,104},{48,112},{56,120},{... | collective-permute-start | bytes 1572872 | tf_op jit(solution)/shard_map/ppermute | solution.py:20
  51.7 29.3 %collective-permute-start.4 = (bf16[16,256,128]{2,1,0:T(8,128)(2,1)S(1)}, bf16[16,256,128]{2,1,0:T(8,128)(2,1)S(1)}, u32[]{:S(2)}, u32[]{:S(2)}) collective-permute-start(bf16[16,256,128]{2,1,0:T(8,128)(2,1)S(1)} %bitcast.53), channel_id=1, source_target_pairs={{0,128},{8,136},{16,144},{24,152},{32,160},{40,168},{48,176},{56,1... | collective-permute-start | bytes 3145736 | tf_op jit(solution)/shard_map/ppermute | solution.py:20
  62.5 20.6 %all-to-all-start = ((s32[32,48,1]{1,2,0:T(1,128)}), s32[32,48,1]{1,2,0:T(1,128)S(1)}, u32[]{:S(2)}, u32[]{:S(2)}) async-start(s32[32,48,1]{1,2,0:T(1,128)} %bitcast.2), calls=%async_computation | async-start | bytes 32768 | tf_op jit(solution)/shard_map/all_to_all | solution.py:68
  83.1 34.5 %all-to-all-start.3 = ((bf16[8,1024,128]{2,1,0:T(8,128)(2,1)}), bf16[8,1024,128]{2,1,0:T(8,128)(2,1)S(1)}, u32[]{:S(2)}, u32[]{:S(2)}) async-start(bf16[8,1024,128]{2,1,0:T(8,128)(2,1)} %bitcast.23), calls=%async_computation.3 | async-start | bytes 4194304 | tf_op jit(solution)/shard_map/all_to_all | solution.py:95
  117.6 70.6 %all-to-all-start.2 = ((bf16[8,1024,128]{2,1,0:T(8,128)(2,1)}), bf16[8,1024,128]{2,1,0:T(8,128)(2,1)}, u32[]{:S(2)}, u32[]{:S(2)}) async-start(bf16[8,1024,128]{2,1,0:T(8,128)(2,1)} %bitcast.55), calls=%async_computation.2 | async-start | bytes 4194304 | tf_op jit(solution)/shard_map/all_to_all | solution.py:94
  181.8 16.8 %copy-start.1 = (s32[256]{0:T(256)S(1)}, s32[256]{0:T(256)}, u32[]{:S(2)}) copy-start(s32[256]{0:T(256)} %param.16) | copy-start | bytes 3076
  181.8 16.8 %copy-start.3 = (bf16[1024]{0:T(1024)(128)(2,1)S(1)}, bf16[1024]{0:T(1024)(128)(2,1)}, u32[]{:S(2)}) copy-start(bf16[1024]{0:T(1024)(128)(2,1)} %param.17) | copy-start | bytes 6148
  188.2 150.3 %all-to-all-start.1 = ((f32[32,48,1024]{2,1,0:T(8,128)}), f32[32,48,1024]{2,1,0:T(8,128)}, u32[]{:S(2)}, u32[]{:S(2)}) async-start(f32[32,48,1024]{2,1,0:T(8,128)} %bitcast.50), calls=%async_computation.1 | async-start | bytes 12582912 | tf_op jit(solution)/shard_map/all_to_all | solution.py:67
  198.5 140.1 %copy-start.4 = (bf16[256,1024]{1,0:T(8,128)(2,1)S(1)}, bf16[256,1024]{1,0:T(8,128)(2,1)}, u32[]{:S(2)}) copy-start(bf16[256,1024]{1,0:T(8,128)(2,1)} %param.15) | copy-start | bytes 1572868
  198.5 200.3 %reduce-scatter.2.cloned.1.call-start = ((), (), s32[]{:S(2)}) async-start(), calls=%async_computation.7 | async-start | bytes 2359296 | tf_op jit(solution)/shard_map/reduce_scatter | solution.py:105
  210.5 152.6 %copy-start.5 = (bf16[128]{0:T(256)(128)(2,1)S(1)}, bf16[128]{0:T(256)(128)(2,1)}, u32[]{:S(2)}) copy-start(bf16[128]{0:T(256)(128)(2,1)} %param.21) | copy-start | bytes 772
  210.5 152.6 %copy-start.6 = (bf16[128]{0:T(256)(128)(2,1)S(1)}, bf16[128]{0:T(256)(128)(2,1)}, u32[]{:S(2)}) copy-start(bf16[128]{0:T(256)(128)(2,1)} %param.20) | copy-start | bytes 772
  344.8 56.5 %copy-start = (bf16[256,1024]{1,0:T(8,128)(2,1)}, bf16[256,1024]{1,0:T(8,128)(2,1)S(1)}, u32[]{:S(2)}) copy-start(bf16[256,1024]{1,0:T(8,128)(2,1)S(1)} %fusion.39) | copy-start | bytes 1572868
Sparse Core Ops, SparseCore 0:
  10.6 85.2 all-gather.4
  97.7 52.1 all-gather.2
  363.2 35.5 reduce-scatter.1
